TPU v7x, 32 devices: a whole 2x2x4 slice. The times are simulated.
32 devices in a mesh: dp: 8 (over y, x, core), mp: 4 (over z).
Axes of the slice: x: 2, y: 2, z: 4, core: 2. Of those that a mesh axis runs over, the one named last changes fastest.
Arguments:
- layer_inputs: bfloat16 [2, 3072, 1024], P(None, 'dp'), may hold values from -11 to 11, as said below
- out_grads: bfloat16 [2, 3072, 1024], P(None, 'dp'), may hold values from -11 to 11, as said below
- damping: float32 [4], replicated, may hold values from 0.1 to 0.5
- owners: int32 [4], replicated, may hold values from 0 to 8, as said below
- old_inverse: bfloat16 [4, 1024, 1024], P('mp'), may hold values from -1.5 to 1.5, as said below
- step_size: float32 [2], replicated, may hold values from 100 to 400
Outputs:
- updates: bfloat16 [2, 1024, 1024], P(None, 'dp')
Inputs may be any that keep to these rules, and one draw needn't show every extreme that they name: `layer_inputs`: layer inputs: rows of mixed scale. `out_grads`: output gradients: rows of mixed scale. `old_inverse`: each kept inverse is symmetric. `owners`: exactly one factor has the value 8.
All inputs are finite; a program needn't handle non-finite values.
Results may differ from a plain program's by a relative error of at most 0.012.
Values may be sent and summed in bfloat16 or wider, within the bound.
A program may use at most 128 MiB of HBM per device.

v0:
```python
import jax
import jax.numpy as jnp
from jax import lax
from jax.sharding import PartitionSpec as P


def invert_damped(factor, shift):
    identity = jnp.eye(factor.shape[0], dtype=jnp.float32)
    lower = jnp.linalg.cholesky(factor + shift * identity)
    return jax.scipy.linalg.cho_solve((lower, True), identity).astype(jnp.bfloat16)


def body(layer_inputs, out_grads, damping, owners, old_inverse, step_size):
    parts_model = lax.axis_size("mp")
    parts_data = lax.axis_size("dp")
    column = lax.axis_index("mp")
    layers = layer_inputs.shape[0]
    full_width = layer_inputs.shape[2]
    block_width = full_width // parts_model
    row_width = full_width // parts_data
    count_all = layer_inputs.shape[1] * parts_data
    inputs_cols = lax.dynamic_slice_in_dim(layer_inputs, column * block_width, block_width, 2)
    grads_cols = lax.dynamic_slice_in_dim(out_grads, column * block_width, block_width, 2)
    input_stats = (
        jnp.einsum("ltd,lte->lde", layer_inputs, inputs_cols, preferred_element_type=jnp.float32)
        / count_all
    )
    grad_stats = (
        jnp.einsum("ltd,lte->lde", out_grads, grads_cols, preferred_element_type=jnp.float32)
        / count_all
    )
    stats_cols = jnp.stack([input_stats, grad_stats], axis=1).reshape(
        2 * layers, full_width, block_width
    )
    grad_rows = (
        jnp.einsum("ltr,ltd->lrd", grads_cols, layer_inputs, preferred_element_type=jnp.float32)
        / count_all
    )
    summed_cols, gradient = lax.psum((stats_cols, grad_rows), "dp")
    factors = lax.all_to_all(summed_cols, "mp", split_axis=0, concat_axis=2, tiled=True)
    local_count = old_inverse.shape[0]
    factor_id = column * local_count + 0
    shift = damping[factor_id]
    owner = owners[factor_id]
    refreshed = owner < parts_data
    local_factor = factors[0]
    kept = old_inverse[0]
    current_list = [lax.cond(refreshed, lambda: invert_damped(local_factor, shift), lambda: kept)]
    inverses = lax.all_gather(jnp.stack(current_list), "mp", axis=0, tiled=True)
    input_inverse = inverses[0::2]
    grad_inverse = inverses[1::2]
    gradient_low = gradient.astype(jnp.bfloat16)
    half_rows = jnp.einsum(
        "lrd,lde->lre", gradient_low, input_inverse, preferred_element_type=jnp.float32
    ).astype(jnp.bfloat16)
    halves = lax.all_gather(half_rows, "mp", axis=1, tiled=True)
    scaled = step_size[:, None, None]
    left_rows = lax.dynamic_slice_in_dim(
        grad_inverse, lax.axis_index("dp") * row_width, row_width, 1
    )
    half_cols = lax.dynamic_slice_in_dim(halves, column * block_width, block_width, 2)
    update_part = (
        jnp.einsum("lrd,lde->lre", left_rows, half_cols, preferred_element_type=jnp.float32)
        * scaled
    ).astype(jnp.bfloat16)
    return lax.all_gather(update_part, "mp", axis=2, tiled=True)


def solution(mesh):
    placed = (P(None, "dp", None), P(None, "dp", None), P(), P(), P("mp", None, None), P())
    return jax.shard_map(
        body, mesh=mesh, in_specs=placed, out_specs=P(None, "dp", None), check_vma=False
    )
```

profile of v0, /device:TPU:0, one launch (start us, length us, event | category | flops | bytes accessed | tf_op | source)
XLA Modules:
  0.0 867.9 jit_solution(7141201046924968040)
XLA Ops:
  6.5 3.3 copy.129
  11.4 2.3 pad_maximum_fusion
  13.7 5.4 copy.47
  19.1 83.9 %all-reduce.4.cloned.1.call-done = f32[4,1024,256]{2,1,0:T(8,128)} async-done(((f32[4,1024,256]{2,1,0:T(8,128)}), f32[4,1024,256]{2,1,0:T(8,128)}) %all-reduce.4.cloned.1.call-update) | async-done | bytes 4194320 | tf_op jit(solution)/shard_map/psum | solution.py:39
  102.9 4.9 all-to-all-start
  109.1 92.1 %all-to-all-done = f32[4,1024,256]{2,1,0:T(8,128)} async-done(((f32[4,1024,256]{2,1,0:T(8,128)}), f32[4,1024,256]{2,1,0:T(8,128)}, u32[]{:S(2)}, u32[]{:S(2)}) %all-to-all-start) | async-done | bytes 4194336 | tf_op jit(solution)/shard_map/all_to_all | solution.py:40
  201.2 410.2 %conditional.1 = (bf16[1024,1024]{1,0:T(8,128)(2,1)}) conditional(s32[]{:T(128)} %bitcast.26, (bf16[1,1024,1024]{2,1,0:T(8,128)(2,1)}) %tuple.64, (f32[1,1024,4,256]{3,1,2,0:T(8,128)}, f32[4]{0:T(128)S(1)}, s32[]{:T(128)}) %tuple.73), branch_computations={%region_1.0_spmd, %region_2.19_spmd} | conditional | flops 17339023360 | bytes 217064480 | solution.py:48
  201.2 5.4 copy.48
  207.2 5.5 bitcast_add_fusion.1
  212.7 5.5 copy.28
  218.2 5.1 fusion
  223.3 2.0 copy-done.2
  225.3 11.7 %cholesky.5 = f32[128,128]{1,0:T(8,128)S(1)} custom-call(f32[128,128]{1,0:T(8,128)S(1)} %cholesky.221), custom_call_target="Cholesky" | custom-call | tf_op jit(solution)/shard_map/cond/branch_1_fun/jit(cholesky)/cholesky | solution.py:9
  237.0 9.8 %custom-call.58 = f32[1,128,128]{1,2,0:T(8,128)S(1)} custom-call(f32[1,128,128]{2,1,0:T(8,128)S(1)} %get-tuple-element.86), custom_call_target="InvertDiagBlocksLowerTriangular" | custom-call | tf_op jit(solution)/shard_map/cond/branch_1_fun/jit(cholesky)/cholesky | solution.py:9
  251.5 11.7 %cholesky.27 = f32[128,128]{1,0:T(8,128)S(1)} custom-call(f32[128,128]{1,0:T(8,128)S(1)} %cholesky.227), custom_call_target="Cholesky" | custom-call | tf_op jit(solution)/shard_map/cond/branch_1_fun/jit(cholesky)/cholesky | solution.py:9
  263.3 2.4 copy.30
  265.9 2.5 cholesky.37
  269.9 9.8 %custom-call.59 = f32[1,128,128]{1,2,0:T(8,128)S(1)} custom-call(f32[1,128,128]{2,1,0:T(8,128)S(1)} %get-tuple-element.84), custom_call_target="InvertDiagBlocksLowerTriangular" | custom-call | tf_op jit(solution)/shard_map/cond/branch_1_fun/jit(cholesky)/cholesky | solution.py:9
  279.7 2.3 convolution_dynamic-update-slice_fusion
  282.1 2.7 convolution_subtract_fusion.11
  285.5 11.7 %cholesky.58 = f32[128,128]{1,0:T(8,128)S(1)} custom-call(f32[128,128]{1,0:T(8,128)S(1)} %cholesky.232), custom_call_target="Cholesky" | custom-call | tf_op jit(solution)/shard_map/cond/branch_1_fun/jit(cholesky)/cholesky | solution.py:9
  301.3 9.8 %custom-call.60 = f32[1,128,128]{1,2,0:T(8,128)S(1)} custom-call(f32[1,128,128]{2,1,0:T(8,128)S(1)} %get-tuple-element.82), custom_call_target="InvertDiagBlocksLowerTriangular" | custom-call | tf_op jit(solution)/shard_map/cond/branch_1_fun/jit(cholesky)/cholesky | solution.py:9
  311.1 2.2 convolution_dynamic-update-slice_fusion.1
  313.3 3.3 convolution_subtract_fusion.12
  317.4 11.7 %cholesky.87 = f32[128,128]{1,0:T(8,128)S(1)} custom-call(f32[128,128]{1,0:T(8,128)S(1)} %cholesky.237), custom_call_target="Cholesky" | custom-call | tf_op jit(solution)/shard_map/cond/branch_1_fun/jit(cholesky)/cholesky | solution.py:9
  331.1 9.8 %custom-call.61 = f32[1,128,128]{1,2,0:T(8,128)S(1)} custom-call(f32[1,128,128]{2,1,0:T(8,128)S(1)} %get-tuple-element.80), custom_call_target="InvertDiagBlocksLowerTriangular" | custom-call | tf_op jit(solution)/shard_map/cond/branch_1_fun/jit(cholesky)/cholesky | solution.py:9
  340.9 2.1 convolution_dynamic-update-slice_fusion.2
  343.0 3.2 convolution_subtract_fusion.13
  346.2 12.1 %cholesky.116 = f32[128,128]{1,0:T(8,128)S(1)} custom-call(f32[128,128]{1,0:T(8,128)S(1)} %cholesky.242), custom_call_target="Cholesky" | custom-call | tf_op jit(solution)/shard_map/cond/branch_1_fun/jit(cholesky)/cholesky | solution.py:9
  361.0 10.6 %custom-call.62 = f32[1,128,128]{1,2,0:T(8,128)S(1)} custom-call(f32[1,128,128]{2,1,0:T(8,128)} %get-tuple-element.78), custom_call_target="InvertDiagBlocksLowerTriangular" | custom-call | tf_op jit(solution)/shard_map/cond/branch_1_fun/jit(cholesky)/cholesky | solution.py:9
  372.7 3.2 convolution_subtract_fusion.14
  376.0 11.7 %cholesky.146 = f32[128,128]{1,0:T(8,128)S(1)} custom-call(f32[128,128]{1,0:T(8,128)S(1)} %cholesky.249), custom_call_target="Cholesky" | custom-call | tf_op jit(solution)/shard_map/cond/branch_1_fun/jit(cholesky)/cholesky | solution.py:9
  389.7 9.8 %custom-call.63 = f32[1,128,128]{1,2,0:T(8,128)S(1)} custom-call(f32[1,128,128]{2,1,0:T(8,128)S(1)} %get-tuple-element.76), custom_call_target="InvertDiagBlocksLowerTriangular" | custom-call | tf_op jit(solution)/shard_map/cond/branch_1_fun/jit(cholesky)/cholesky | solution.py:9
  400.6 2.9 convolution_subtract_fusion.15
  403.5 11.7 %cholesky.176 = f32[128,128]{1,0:T(8,128)S(1)} custom-call(f32[128,128]{1,0:T(8,128)S(1)} %cholesky.256), custom_call_target="Cholesky" | custom-call | tf_op jit(solution)/shard_map/cond/branch_1_fun/jit(cholesky)/cholesky | solution.py:9
  417.3 9.8 %custom-call.64 = f32[1,128,128]{1,2,0:T(8,128)S(1)} custom-call(f32[1,128,128]{2,1,0:T(8,128)S(1)} %get-tuple-element.74), custom_call_target="InvertDiagBlocksLowerTriangular" | custom-call | tf_op jit(solution)/shard_map/cond/branch_1_fun/jit(cholesky)/cholesky | solution.py:9
  428.0 2.2 convolution_subtract_fusion.16
  430.2 11.7 %cholesky.204 = f32[128,128]{1,0:T(8,128)S(1)} custom-call(f32[128,128]{1,0:T(8,128)S(1)} %convolution_subtract_fusion.16), custom_call_target="Cholesky" | custom-call | tf_op jit(solution)/shard_map/cond/branch_1_fun/jit(cholesky)/cholesky | solution.py:9
  444.0 4.9 select_select_fusion
  448.9 28.2 %while.1 = (s32[]{:T(128)}, f32[1024,1024]{0,1:T(8,128)}, s32[8,2]{0,1:T(2,128)S(1)}, f32[8,128,128]{2,1,0:T(8,128)}, s32[]{:T(128)}) while((s32[]{:T(128)}, f32[1024,1024]{0,1:T(8,128)}, s32[8,2]{0,1:T(2,128)S(1)}, f32[8,128,128]{2,1,0:T(8,128)}, s32[]{:T(128)}) %tuple.61), condition=%wide.while_cond, body=%wide.while_body.sunk | while | flops 2 | bytes 393829 | solution.py:10
  449.5 2.2 dynamic-slice.7
  453.0 2.2 dynamic-slice.7
  456.6 2.2 dynamic-slice.7
  460.1 2.2 dynamic-slice.7
  463.6 2.2 dynamic-slice.7
  467.2 2.2 dynamic-slice.7
  470.7 2.2 dynamic-slice.7
  474.2 2.1 dynamic-slice.7
  477.1 80.4 %custom-call.65 = f32[8,128,128]{1,2,0:T(8,128)} custom-call(f32[8,128,128]{2,1,0:T(8,128)} %get-tuple-element.34), custom_call_target="InvertDiagBlocksLowerTriangular" | custom-call | tf_op jit(solution)/shard_map/cond/branch_1_fun/jit(_cho_solve)/triangular_solve | solution.py:10
  561.6 1.8 convolution_subtract_fusion.1
  564.2 2.8 fusion.33
  567.7 3.5 fusion.39
  572.1 4.4 convolution_subtract_fusion.5
  577.2 5.1 convolution_subtract_fusion.3
  583.0 6.3 convolution_subtract_fusion.8
  596.9 1.9 convolution_subtract_fusion.4
  602.4 2.2 convolution_subtract_fusion.6
  611.5 2.2 convolution_multiply_fusion
  613.6 58.2 %all-reduce.5 = bf16[2,256,1024]{2,1,0:T(8,128)(2,1)S(1)} all-reduce(f32[2,256,1024]{2,1,0:T(8,128)} %convolution_multiply_fusion), channel_id=1, replica_groups=mesh['dp'=8,'mp'=4] {'dp'}, use_global_device_ids=true, to_apply=%region_19.20 | all-reduce | flops 524288 | bytes 3145728 | tf_op jit(solution)/shard_map/psum | solution.py:39
  671.9 86.8 %all-gather.6.cloned.1.call-done = bf16[4096,1024]{1,0:T(8,128)(2,1)} async-done(((bf16[1024,1024]{1,0:T(8,128)(2,1)}), bf16[4096,1024]{1,0:T(8,128)(2,1)}) %all-gather.6.cloned.1.call-update) | async-done | bytes 8388624 | tf_op jit(solution)/shard_map/all_gather | solution.py:49
  758.7 4.4 fusion.114
  763.1 4.6 slice.321
  767.7 74.5 %all-gather.4.cloned.1.call-done = bf16[2,1024,1024]{2,1,0:T(8,128)(2,1)} async-done(((bf16[2,256,1024]{2,1,0:T(8,128)(2,1)}), bf16[2,1024,1024]{2,1,0:T(8,128)(2,1)}) %all-gather.4.cloned.1.call-update) | async-done | bytes 4194320 | tf_op jit(solution)/shard_map/all_gather | solution.py:56
  844.0 16.1 %all_gather.11 = bf16[2,128,1024]{2,1,0:T(8,128)(2,1)S(1)} all-gather(bf16[2,128,256]{2,1,0:T(8,128)(2,1)S(1)} %fusion.117), channel_id=1, replica_groups=mesh['dp'=8,'mp'=4] {'mp'}, dimensions={2}, use_global_device_ids=true | all-gather | bytes 655360 | tf_op jit(solution)/shard_map/all_gather | solution.py:66
  (161 shorter events, 61.9 us)
Async XLA Ops:
  6.5 3.3 copy-start
  6.5 4.0 copy-start.3
  6.5 96.4 %all-reduce.4.cloned.1.call-start = ((), (), s32[]{:S(2)}) async-start(), calls=%async_computation.1 | async-start | bytes 8388608 | tf_op jit(solution)/shard_map/psum | solution.py:39
  19.1 88.8 %copy-start.11 = (s32[4]{0:T(128)S(1)}, s32[4]{0:T(128)}, u32[]{:S(2)}) copy-start(s32[4]{0:T(128)} %param.11) | copy-start | bytes 52
  19.1 182.1 %copy-start.12 = (f32[4]{0:T(128)S(1)}, f32[4]{0:T(128)}, u32[]{:S(2)}) copy-start(f32[4]{0:T(128)} %param.10) | copy-start | bytes 52
  102.9 98.3 %all-to-all-start = ((f32[4,1024,256]{2,1,0:T(8,128)}), f32[4,1024,256]{2,1,0:T(8,128)}, u32[]{:S(2)}, u32[]{:S(2)}) async-start(f32[4,1024,256]{2,1,0:T(8,128)} %all-reduce.4.cloned.1.call-done), calls=%async_computation | async-start | bytes 8388608 | tf_op jit(solution)/shard_map/all_to_all | solution.py:40
  107.8 650.9 %all-gather.6.cloned.1.call-start = ((), (), s32[]{:S(2)}) async-start(), calls=%async_computation.3 | async-start | bytes 10485760 | tf_op jit(solution)/shard_map/all_gather | solution.py:49
  223.3 2.0 copy-start.2
  248.4 0.8 copy-start.4
  250.7 0.8 copy-start.7
  265.9 2.5 copy-start.6
  284.8 0.7 copy-start.8
  316.6 0.7 copy-start.9
  557.5 2.4 copy-start.1
  557.8 3.0 copy-start.5
  611.4 230.8 %all-gather.4.cloned.1.call-start = ((), (), s32[]{:S(2)}) async-start(), calls=%async_computation.2 | async-start | bytes 5242880 | tf_op jit(solution)/shard_map/all_gather | solution.py:56
  763.1 79.1 %copy-start.10 = (f32[2]{0:T(128)S(1)}, f32[2]{0:T(128)}, u32[]{:S(2)}) copy-start(f32[2]{0:T(128)} %param.13) | copy-start | bytes 28
Sparse Core Ops, SparseCore 0:
  19.2 83.7 all-reduce.3
  611.5 147.0 all-gather.5
  763.2 78.9 all-gather.3
where the time goes:
time: 873 us; the launch traced here: 868 us
  waiting for transfers between devices  337 us (39%)
  other arithmetic  272 us (31%)
  matrix products  86.6 us (10%)
  blocking collectives  74.4 us (9%)
  local copies, waits for them, and re-layouts  71.7 us (8%)
  between operations  14.4 us (2%)
    another operation x30, other arithmetic, invert_damped(): lower = jnp.linalg.cholesky(factor + shift * identity)  169 us
    all_to_all x1, waiting for transfers between devices, body(): lax.all_to_all(summed_cols, 'mp', split_axis=0, concat_axis=2, tiled=True)  92.1 us
    all_gather x1, waiting for transfers between devices, body(): inverses = lax.all_gather(jnp.stack(current_list), 'mp', axis=0, tiled=True)  86.8 us
    another operation x4, other arithmetic, invert_damped(): jax.scipy.linalg.cho_solve((lower, True), identity).astype(jnp.bfloat16)  86 us
    psum x1, waiting for transfers between devices, body(): summed_cols, gradient = lax.psum((stats_cols, grad_rows), 'dp')  83.9 us
    all_gather x1, waiting for transfers between devices, body(): halves = lax.all_gather(half_rows, 'mp', axis=1, tiled=True)  74.5 us
    psum x1, blocking collectives, body(): summed_cols, gradient = lax.psum((stats_cols, grad_rows), 'dp')  58.2 us
    another operation x30, matrix products, invert_damped(): jax.scipy.linalg.cho_solve((lower, True), identity).astype(jnp.bfloat16)  46.5 us
  transfers between devices with their start and end apart: 4, of which 4 were waited for; matrix products, arithmetic and copies ran while one was open for 1% of the time, Pallas kernels for 0%

commit v1 on v0

v1 whole, which is shorter than its diff:
```python
import functools
import jax
import jax.numpy as jnp
from jax import lax
from jax.experimental import pallas as pl
from jax.experimental.pallas import tpu as pltpu
from jax.sharding import PartitionSpec as P

F32 = jnp.float32
BF16 = jnp.bfloat16
MESH = pl.DeviceIdType.MESH
HI = lax.Precision.HIGHEST
BLOCK = 128
TILE = 8


def remote(src, dst, send, recv, where):
    return pltpu.make_async_remote_copy(
        src_ref=src, dst_ref=dst, send_sem=send, recv_sem=recv,
        device_id=where, device_id_type=MESH,
    )


def gather_kernel(n, x, y, gx, gy, loc, s1, r1, s2, r2, s3, r3):
    me = lax.axis_index("dp")
    m = lax.axis_index("mp")
    half = n // 2
    pair, side = me // 2, me % 2
    sibling = pair * 2 + 1 - side
    barrier = pltpu.get_barrier_semaphore()
    for s in range(1, n):
        pl.semaphore_signal(barrier, inc=1, device_id=((me + s) % n, m), device_id_type=MESH)
    pl.semaphore_wait(barrier, n - 1)

    sent = []
    for s in range(1, half):
        peer = ((pair + s) % half) * 2 + side
        c = remote(x, gx.at[me], s1.at[s], r1.at[s], (peer, m))
        c.start()
        sent.append(c)
    own = remote(x, gx.at[me], s1.at[0], r1.at[0], (sibling, m))
    own.start()
    sent.append(own)
    blocks = []
    for s in range(1, n):
        peer = (me + s) % n
        c = remote(y.at[peer], gy.at[me], s3.at[s], r3.at[s], (peer, m))
        c.start()
        sent.append(c)
        blocks.append((s, (me - s + n) % n))
    here = pltpu.make_async_copy(x, gx.at[me], loc.at[0])
    here.start()
    here_y = pltpu.make_async_copy(y.at[me], gy.at[me], loc.at[1])
    here_y.start()
    for s in range(1, half):
        origin = ((pair - s + half) % half) * 2 + side
        remote(x, gx.at[origin], s1.at[s], r1.at[s], (sibling, m)).wait_recv()
        c = remote(gx.at[origin], gx.at[origin], s2.at[s], r2.at[s], (sibling, m))
        c.start()
        sent.append(c)
    remote(x, gx.at[sibling], s1.at[0], r1.at[0], (sibling, m)).wait_recv()
    for s in range(1, half):
        origin = ((pair - s + half) % half) * 2 + 1 - side
        remote(x, gx.at[origin], s2.at[s], r2.at[s], (sibling, m)).wait_recv()
    for s, origin in blocks:
        remote(y.at[origin], gy.at[origin], s3.at[s], r3.at[s], (origin, m)).wait_recv()
    for c in sent:
        c.wait_send()
    here.wait()
    here_y.wait()


def gather(n, x, y):
    any_space = pl.BlockSpec(memory_space=pl.ANY)
    dma = pltpu.SemaphoreType.DMA
    return pl.pallas_call(
        functools.partial(gather_kernel, n),
        out_shape=[
            jax.ShapeDtypeStruct((n,) + x.shape, x.dtype),
            jax.ShapeDtypeStruct(y.shape, y.dtype),
        ],
        in_specs=[any_space] * 2,
        out_specs=[any_space] * 2,
        scratch_shapes=[dma((2,)), dma((n,)), dma((n,)), dma((n,)), dma((n,)), dma((n,)), dma((n,))],
        compiler_params=pltpu.CompilerParams(collective_id=0, has_side_effects=True),
        name="gather_sources",
    )(x, y)


def sweep_block(tiles):
    width = tiles[0].shape[1]
    lane = lax.broadcasted_iota(jnp.int32, (TILE, width), 1)
    sub = lax.broadcasted_iota(jnp.int32, (TILE, width), 0)
    for k in range(width):
        kt, ks = divmod(k, TILE)
        row = jnp.broadcast_to(tiles[kt][ks : ks + 1, :], (TILE, width))
        pivot = jnp.broadcast_to(row[:, k : k + 1], (TILE, width))
        inv = 1.0 / pivot
        at = lane == k
        scaled = jnp.where(at, -inv, row * inv)
        out = []
        for t, tile in enumerate(tiles):
            col = jnp.broadcast_to(tile[:, k : k + 1], (TILE, width))
            new = jnp.where(at, 0.0, tile) - col * scaled
            if t == kt:
                new = jnp.where(sub == ks, scaled, new)
            out.append(new)
        tiles = out
    return tiles


def invert_kernel(refreshed, shift, factor, kept, out, a, r, p):
    width = factor.shape[0]
    steps = width // BLOCK
    row_id = lax.broadcasted_iota(jnp.int32, (BLOCK, width), 0)
    col_id = lax.broadcasted_iota(jnp.int32, (BLOCK, width), 1)

    @pl.loop(0, steps)
    def _(i):
        rows = pl.ds(pl.multiple_of(i * BLOCK, BLOCK), BLOCK)
        a[rows, :] = factor[rows, :] + jnp.where(row_id + i * BLOCK == col_id, shift[0], 0.0)

    @pl.loop(0, steps)
    def _(k):
        ks = pl.ds(pl.multiple_of(k * BLOCK, BLOCK), BLOCK)
        block = a[ks, ks]
        tiles = [block[t * TILE : (t + 1) * TILE, :] for t in range(BLOCK // TILE)]
        tiles = sweep_block(tiles)
        for t, tile in enumerate(tiles):
            p[t * TILE : (t + 1) * TILE, :] = tile
        r[...] = -jnp.dot(p[...], a[ks, :], precision=HI, preferred_element_type=F32)

        @pl.loop(0, steps)
        def _(i):
            rows = pl.ds(pl.multiple_of(i * BLOCK, BLOCK), BLOCK)
            c = a[rows, ks]
            a[rows, :] = a[rows, :] - jnp.dot(c, r[...], precision=HI, preferred_element_type=F32)
            a[rows, ks] = -jnp.dot(c, p[...], precision=HI, preferred_element_type=F32)

        a[ks, :] = r[...]
        a[ks, ks] = p[...]

    fresh = refreshed[0] > 0

    @pl.loop(0, steps)
    def _(i):
        rows = pl.ds(pl.multiple_of(i * BLOCK, BLOCK), BLOCK)
        out[rows, :] = jnp.where(fresh, -a[rows, :], kept[rows, :].astype(F32)).astype(BF16)


def invert(refreshed, shift, factor, kept):
    width = factor.shape[0]
    smem = pl.BlockSpec(memory_space=pltpu.SMEM)
    vmem = pl.BlockSpec(memory_space=pltpu.VMEM)
    return pl.pallas_call(
        invert_kernel,
        out_shape=jax.ShapeDtypeStruct((width, width), BF16),
        in_specs=[smem, smem, vmem, vmem],
        out_specs=vmem,
        scratch_shapes=[
            pltpu.VMEM((width, width), F32),
            pltpu.VMEM((BLOCK, width), F32),
            pltpu.VMEM((BLOCK, BLOCK), F32),
        ],
        compiler_params=pltpu.CompilerParams(vmem_limit_bytes=40 * 1024 * 1024),
        name="invert_damped",
    )(refreshed, shift, factor, kept)


def apply_kernel(n, parts, inv, grad, step, out, b, got, done, s1, r1, s2, r2):
    me = lax.axis_index("dp")
    m = lax.axis_index("mp")
    other = m + 1 - 2 * (m % 2)
    width = inv.shape[0]
    rw = width // n
    is_out = m % 2
    barrier = pltpu.get_barrier_semaphore()
    for j in range(n):
        pl.semaphore_signal(barrier, inc=1, device_id=(j, other), device_id_type=MESH)
    for q in range(1, parts):
        pl.semaphore_signal(barrier, inc=1, device_id=(me, (m + q) % parts), device_id_type=MESH)
    pl.semaphore_wait(barrier, n + parts - 1)

    b[...] = jnp.dot(inv[...], grad[...], preferred_element_type=F32).astype(BF16).reshape(n, rw, rw)
    for s in range(n):
        j = (me + s) % n

        @pl.when(is_out == 1)
        def _():
            remote(b.at[j], got.at[me], s1.at[s], r1.at[s], (j, other)).start()

    @pl.when(is_out == 0)
    def _():
        for s in range(n):
            origin = (me - s + n) % n
            remote(b.at[origin], got.at[origin], s1.at[s], r1.at[s], (origin, other)).wait_recv()
        total = jnp.zeros((rw, width), F32)
        for j in range(n):
            total = total + jnp.dot(got[j], inv[j * rw : (j + 1) * rw, :], preferred_element_type=F32)
        done[m // 2] = (total * step[m // 2]).astype(BF16)
        for q in range(1, parts):
            remote(
                done.at[m // 2], done.at[m // 2], s2.at[q], r2.at[q], (me, (m + q) % parts)
            ).start()
        for q in range(1, parts):
            remote(
                done.at[m // 2], done.at[m // 2], s2.at[q], r2.at[q], (me, (m + q) % parts)
            ).wait_send()

    @pl.when(is_out == 1)
    def _():
        for s in range(n):
            j = (me + s) % n
            remote(b.at[j], got.at[me], s1.at[s], r1.at[s], (j, other)).wait_send()

    for q in range(1, parts):
        origin = (m - q + parts) % parts

        @pl.when(origin % 2 == 0)
        def _():
            slot = origin // 2
            remote(done.at[slot], done.at[slot], s2.at[q], r2.at[q], (me, origin)).wait_recv()

    out[...] = done[...]


def apply(n, parts, inv, grad, step):
    width = inv.shape[0]
    rw = width // n
    layers = step.shape[0]
    vmem = pl.BlockSpec(memory_space=pltpu.VMEM)
    dma = pltpu.SemaphoreType.DMA
    return pl.pallas_call(
        functools.partial(apply_kernel, n, parts),
        out_shape=jax.ShapeDtypeStruct((layers, rw, width), BF16),
        in_specs=[vmem, vmem, pl.BlockSpec(memory_space=pltpu.SMEM)],
        out_specs=vmem,
        scratch_shapes=[
            pltpu.VMEM((n, rw, rw), BF16),
            pltpu.VMEM((n, rw, rw), BF16),
            pltpu.VMEM((layers, rw, width), BF16),
            dma((n,)), dma((n,)), dma((parts,)), dma((parts,)),
        ],
        compiler_params=pltpu.CompilerParams(
            collective_id=1, has_side_effects=True, vmem_limit_bytes=32 * 1024 * 1024
        ),
        name="apply_inverses",
    )(inv, grad, step)


def body(layer_inputs, out_grads, damping, owners, old_inverse, step_size):
    parts = lax.axis_size("mp")
    n = lax.axis_size("dp")
    m = lax.axis_index("mp")
    tokens = layer_inputs.shape[1]
    width = layer_inputs.shape[2]
    count_all = tokens * n
    rw = width // n
    xs = lax.dynamic_index_in_dim(layer_inputs, m // 2, 0, keepdims=False)
    gs = lax.dynamic_index_in_dim(out_grads, m // 2, 0, keepdims=False)
    even = m % 2 == 0
    mine = jnp.where(even, xs, gs)
    other = jnp.where(even, gs, xs).reshape(tokens, n, rw).transpose(1, 0, 2)
    source, columns = gather(n, mine, other)
    source = source.reshape(count_all, width)
    columns = columns.reshape(count_all, rw)
    dims = (((0,), (0,)), ((), ()))
    factor = lax.dot_general(source, source, dims, preferred_element_type=F32) / count_all
    grad = (lax.dot_general(source, columns, dims, preferred_element_type=F32) / count_all).astype(BF16)
    refreshed = (owners[m] < n).astype(jnp.int32).reshape(1)
    shift = damping[m].reshape(1)
    inverse = invert(refreshed, shift, factor, old_inverse[0])
    return apply(n, parts, inverse, grad, step_size)


def solution(mesh):
    placed = (P(None, "dp", None), P(None, "dp", None), P(), P(), P("mp", None, None), P())
    return jax.shard_map(
        body, mesh=mesh, in_specs=placed, out_specs=P(None, "dp", None), check_vma=False
    )
```

time: 873 us -> 285 us (0.33)
  waiting for transfers between devices: 337 us -> 0 us
  other arithmetic: 272 us -> 2.35 us
  Pallas kernels: 0 us -> 265 us
  matrix products: 86.6 us -> 12 us
  blocking collectives: 74.4 us -> 0 us
  local copies, waits for them, and re-layouts: 71.7 us -> 4.8 us
  between operations: 14.4 us -> 0.75 us
    pallas_call x0 -> x3, Pallas kernels: none -> 265 us  [the longest x1 187 us: invert(): pl.pallas_call(invert_kernel, out_shape=jax.ShapeDtypeStruct((width, widt...]
    another operation x35 -> x0, other arithmetic: 257 us -> none  [the longest x30 169 us: invert_damped(): lower = jnp.linalg.cholesky(factor + shift * identity)]
    all_gather x2 -> x0, waiting for transfers between devices: 161 us -> none  [the longest x1 86.8 us: body(): inverses = lax.all_gather(jnp.stack(current_list), 'mp', axis=0, tiled=True)]
    all_to_all x1 -> x0, waiting for transfers between devices: 92.1 us -> none  [body(): lax.all_to_all(summed_cols, 'mp', split_axis=0, concat_axis=2, tiled=True)]
    psum x1 -> x0, waiting for transfers between devices: 83.9 us -> none  [body(): summed_cols, gradient = lax.psum((stats_cols, grad_rows), 'dp')]
    another operation x44 -> x0, matrix products: 76.8 us -> none  [the longest x30 46.5 us: invert_damped(): jax.scipy.linalg.cho_solve((lower, True), identity).astype(jnp.bfloat16)]
    psum x1 -> x0, blocking collectives: 58.2 us -> none  [body(): summed_cols, gradient = lax.psum((stats_cols, grad_rows), 'dp')]
    another operation x71 -> x0, local copies, waits for them, and re-layouts: 50.1 us -> none
  transfers between devices with their start and end apart: 4 -> 0, of which waited for: 4 -> 0; matrix products, arithmetic and copies ran while one was open for 1% -> 0% of each run, Pallas kernels for 0% -> 0%
where the time goes in v1:
time: 285 us
  Pallas kernels  265 us (93%)
  matrix products  12 us (4%)
  local copies, waits for them, and re-layouts  4.8 us (2%)
    pallas_call x1, Pallas kernels, invert(): pl.pallas_call(invert_kernel, out_shape=jax.ShapeDtypeStruct((width, widt...  187 us
    pallas_call x1, Pallas kernels, gather(): pl.pallas_call(functools.partial(gather_kernel, n), out_shape=[jax.ShapeD...  47.4 us
    pallas_call x1, Pallas kernels, apply(): pl.pallas_call(functools.partial(apply_kernel, n, parts), out_shape=jax.S...  30.6 us
    dot_general x1, matrix products, body(): lax.dot_general(source, source, dims, preferred_element_type=F32)  7.03 us

profile of v1, /device:TPU:0, one launch (start us, length us, event | category | flops | bytes accessed | tf_op | source)
XLA Modules:
  0.0 284.6 jit_solution(14800782587762968534)
XLA Ops:
  0.0 1.2 dynamic_slice.13
  1.9 1.2 dynamic_slice.14.shift
  3.1 2.3 broadcast_select_fusion
  5.5 0.4 copy.9
  5.8 1.2 copy.10
  7.0 47.4 %gather_sources.1 = (bf16[8,384,1024]{2,1,0:T(8,128)(2,1)}, bf16[8,384,128]{2,1,0:T(8,128)(2,1)}) custom-call(bf16[384,1024]{1,0:T(8,128)(2,1)} %get-tuple-element.10.x, bf16[8,384,128]{2,1,0:T(8,128)(2,1)} %bitcast.18), custom_call_target="tpu_custom_call" | custom-call | tf_op jit(solution)/shard_map/gather_sources/pallas_call | solution.py:76
  54.4 0.0 copy-start.2
  54.4 4.9 %fusion.1.grad = bf16[1024,128]{1,0:T(8,128)(2,1)S(1)} fusion(bf16[8,384,1024]{2,1,0:T(8,128)(2,1)} %get-tuple-element.7, bf16[8,384,128]{2,1,0:T(8,128)(2,1)} %get-tuple-element.8), kind=kOutput, calls=%fused_computation.3 | convolution fusion | flops 805568512 | bytes 7340032 | tf_op jit(solution)/shard_map/dot_general | solution.py:269
  59.3 0.0 copy-done.2
  59.4 0.0 copy-start
  59.4 7.0 %bitcast_multiply_fusion.factor = f32[1024,1024]{1,0:T(8,128)S(1)} fusion(bf16[8,384,1024]{2,1,0:T(8,128)(2,1)S(1)} %copy-done.2), kind=kOutput, calls=%fused_computation | convolution fusion | flops 6443499520 | bytes 10485760 | tf_op jit(solution)/shard_map/dot_general | solution.py:268
  66.4 0.0 copy-done
  66.4 0.0 copy-start.1
  66.4 186.7 %invert_damped.1.inv = bf16[1024,1024]{1,0:T(8,128)(2,1)S(1)} custom-call(s32[1]{0:T(128)S(6)} %convert_element_type.7.refreshed, f32[1]{0:T(128)} %dynamic_slice.14.shift, f32[1024,1024]{1,0:T(8,128)S(1)} %bitcast_multiply_fusion.factor, bf16[1024,1024]{1,0:T(8,128)(2,1)S(1)} %bitcast.17), custom_call_target="tpu_custom_call" | custom-call | tf_op jit(solution)/shard_map/invert_damped/pallas_call | solution.py:155
  253.2 0.0 copy-done.1
  253.2 30.6 %apply_inverses.1 = bf16[2,128,1024]{2,1,0:T(8,128)(2,1)S(1)} custom-call(bf16[1024,1024]{1,0:T(8,128)(2,1)S(1)} %invert_damped.1.inv, bf16[1024,128]{1,0:T(8,128)(2,1)S(1)} %fusion.1.grad, f32[2]{0:T(128)S(1)} %copy-done.1), custom_call_target="tpu_custom_call" | custom-call | tf_op jit(solution)/shard_map/apply_inverses/pallas_call | solution.py:233
  283.8 0.8 copy.16
Async XLA Ops:
  54.4 5.0 %copy-start.2 = (bf16[8,384,1024]{2,1,0:T(8,128)(2,1)S(1)}, bf16[8,384,1024]{2,1,0:T(8,128)(2,1)}, u32[]{:S(2)}) copy-start(bf16[8,384,1024]{2,1,0:T(8,128)(2,1)} %get-tuple-element.7) | copy-start | bytes 18874372
  59.4 7.1 %copy-start = (bf16[1,1024,1024]{2,1,0:T(8,128)(2,1)S(1)}, bf16[1,1024,1024]{2,1,0:T(8,128)(2,1)}, u32[]{:S(2)}) copy-start(bf16[1,1024,1024]{2,1,0:T(8,128)(2,1)} %param.10) | copy-start | bytes 6291460
  66.4 186.7 %copy-start.1 = (f32[2]{0:T(128)S(1)}, f32[2]{0:T(128)}, u32[]{:S(2)}) copy-start(f32[2]{0:T(128)} %step.1) | copy-start | bytes 28

commit v2 on v1

--- a/solution.py
+++ b/solution.py
@@ -21,7 +21,7 @@
     )
 
 
-def gather_kernel(n, x, y, gx, gy, loc, s1, r1, s2, r2, s3, r3):
+def gather_kernel(n, direct, a_ref, b_ref, gx, gy, loc, s1, r1, s2, r2, s3, r3):
     me = lax.axis_index("dp")
     m = lax.axis_index("mp")
     half = n // 2
@@ -32,52 +32,64 @@
         pl.semaphore_signal(barrier, inc=1, device_id=((me + s) % n, m), device_id_type=MESH)
     pl.semaphore_wait(barrier, n - 1)
 
-    sent = []
-    for s in range(1, half):
-        peer = ((pair + s) % half) * 2 + side
-        c = remote(x, gx.at[me], s1.at[s], r1.at[s], (peer, m))
-        c.start()
-        sent.append(c)
-    own = remote(x, gx.at[me], s1.at[0], r1.at[0], (sibling, m))
-    own.start()
-    sent.append(own)
-    blocks = []
-    for s in range(1, n):
-        peer = (me + s) % n
-        c = remote(y.at[peer], gy.at[me], s3.at[s], r3.at[s], (peer, m))
-        c.start()
-        sent.append(c)
-        blocks.append((s, (me - s + n) % n))
-    here = pltpu.make_async_copy(x, gx.at[me], loc.at[0])
-    here.start()
-    here_y = pltpu.make_async_copy(y.at[me], gy.at[me], loc.at[1])
-    here_y.start()
+    def begin(x, part):
+        for s in range(1, half):
+            peer = ((pair + s) % half) * 2 + side
+            remote(x, gx.at[me], s1.at[s], r1.at[s], (peer, m)).start()
+        remote(x, gx.at[me], s1.at[0], r1.at[0], (sibling, m)).start()
+        for s in range(1, n):
+            peer = (me + s) % n
+            remote(part(peer), gy.at[me], s3.at[s], r3.at[s], (peer, m)).start()
+        pltpu.make_async_copy(x, gx.at[me], loc.at[0]).start()
+        pltpu.make_async_copy(part(me), gy.at[me], loc.at[1]).start()
+
+    if direct:
+        layer = m // 2
+        rw = gy.shape[2]
+
+        def columns(ref):
+            return lambda j: ref.at[layer, :, pl.ds(pl.multiple_of(j * rw, rw), rw)]
+
+        @pl.when(m % 2 == 0)
+        def _():
+            begin(a_ref.at[layer], columns(b_ref))
+
+        @pl.when(m % 2 == 1)
+        def _():
+            begin(b_ref.at[layer], columns(a_ref))
+    else:
+        begin(a_ref, lambda j: b_ref.at[j])
+
+    x = gx.at[me]
     for s in range(1, half):
         origin = ((pair - s + half) % half) * 2 + side
         remote(x, gx.at[origin], s1.at[s], r1.at[s], (sibling, m)).wait_recv()
-        c = remote(gx.at[origin], gx.at[origin], s2.at[s], r2.at[s], (sibling, m))
-        c.start()
-        sent.append(c)
+        remote(gx.at[origin], gx.at[origin], s2.at[s], r2.at[s], (sibling, m)).start()
     remote(x, gx.at[sibling], s1.at[0], r1.at[0], (sibling, m)).wait_recv()
     for s in range(1, half):
         origin = ((pair - s + half) % half) * 2 + 1 - side
         remote(x, gx.at[origin], s2.at[s], r2.at[s], (sibling, m)).wait_recv()
-    for s, origin in blocks:
-        remote(y.at[origin], gy.at[origin], s3.at[s], r3.at[s], (origin, m)).wait_recv()
-    for c in sent:
-        c.wait_send()
-    here.wait()
-    here_y.wait()
-
-
-def gather(n, x, y):
+    for s in range(1, n):
+        origin = (me - s + n) % n
+        remote(gy.at[me], gy.at[origin], s3.at[s], r3.at[s], (origin, m)).wait_recv()
+    for s in range(half):
+        remote(x, x, s1.at[s], r1.at[s], (sibling, m)).wait_send()
+    for s in range(1, half):
+        remote(x, x, s2.at[s], r2.at[s], (sibling, m)).wait_send()
+    for s in range(1, n):
+        remote(gy.at[me], gy.at[me], s3.at[s], r3.at[s], (sibling, m)).wait_send()
+    pltpu.make_async_copy(x, x, loc.at[0]).wait()
+    pltpu.make_async_copy(gy.at[me], gy.at[me], loc.at[1]).wait()
+
+
+def gather(n, direct, x, y):
     any_space = pl.BlockSpec(memory_space=pl.ANY)
     dma = pltpu.SemaphoreType.DMA
     return pl.pallas_call(
-        functools.partial(gather_kernel, n),
+        functools.partial(gather_kernel, n, direct),
         out_shape=[
-            jax.ShapeDtypeStruct((n,) + x.shape, x.dtype),
-            jax.ShapeDtypeStruct(y.shape, y.dtype),
+            jax.ShapeDtypeStruct((n,) + x.shape[-2:], x.dtype),
+            jax.ShapeDtypeStruct((n, x.shape[-2], x.shape[-1] // n), y.dtype),
         ],
         in_specs=[any_space] * 2,
         out_specs=[any_space] * 2,
@@ -89,22 +101,60 @@
 
 def sweep_block(tiles):
     width = tiles[0].shape[1]
-    lane = lax.broadcasted_iota(jnp.int32, (TILE, width), 1)
-    sub = lax.broadcasted_iota(jnp.int32, (TILE, width), 0)
-    for k in range(width):
-        kt, ks = divmod(k, TILE)
-        row = jnp.broadcast_to(tiles[kt][ks : ks + 1, :], (TILE, width))
-        pivot = jnp.broadcast_to(row[:, k : k + 1], (TILE, width))
-        inv = 1.0 / pivot
-        at = lane == k
-        scaled = jnp.where(at, -inv, row * inv)
+    shape = (TILE, width)
+    lane = lax.broadcasted_iota(jnp.int32, shape, 1)
+    sub = lax.broadcasted_iota(jnp.int32, shape, 0)
+    idx = range(TILE)
+    for g in range(width // TILE):
+        first = g * TILE
+        inside = (lane >= first) & (lane < first + TILE)
+        rows = [jnp.broadcast_to(tiles[g][i : i + 1, :], shape) for i in idx]
+        s = {
+            (i, j): jnp.broadcast_to(rows[i][:, first + j : first + j + 1], shape)
+            for i in idx for j in idx if i <= j
+        }
+
+        def at(i, j):
+            return (i, j) if i <= j else (j, i)
+
+        for k in idx[::2]:
+            h = k + 1
+            inv = 1.0 / (s[k, k] * s[h, h] - s[k, h] * s[k, h])
+            p00, p01, p11 = s[h, h] * inv, -s[k, h] * inv, s[k, k] * inv
+            rest = [i for i in idx if i not in (k, h)]
+            u = {i: s[at(i, k)] * p00 + s[at(i, h)] * p01 for i in rest}
+            v = {i: s[at(i, k)] * p01 + s[at(i, h)] * p11 for i in rest}
+            for i in rest:
+                for j in rest:
+                    if i <= j:
+                        s[i, j] = s[i, j] - (s[at(i, k)] * u[j] + s[at(i, h)] * v[j])
+            for i in rest:
+                s[at(i, k)] = u[i]
+                s[at(i, h)] = v[i]
+            s[k, k], s[k, h], s[h, h] = -p00, -p01, -p11
+        rows = [
+            jnp.where(inside, jnp.where(lane == first + i, -1.0, 0.0), rows[i]) for i in idx
+        ]
+        scaled = []
+        for i in idx:
+            terms = [s[at(i, j)] * rows[j] for j in idx]
+            while len(terms) > 1:
+                terms = [x + y for x, y in zip(terms[0::2], terms[1::2])]
+            scaled.append(-terms[0])
         out = []
         for t, tile in enumerate(tiles):
-            col = jnp.broadcast_to(tile[:, k : k + 1], (TILE, width))
-            new = jnp.where(at, 0.0, tile) - col * scaled
-            if t == kt:
-                new = jnp.where(sub == ks, scaled, new)
-            out.append(new)
+            if t == g:
+                fresh = scaled[0]
+                for i in idx[1:]:
+                    fresh = jnp.where(sub == i, scaled[i], fresh)
+                out.append(fresh)
+                continue
+            terms = [
+                jnp.broadcast_to(tile[:, first + i : first + i + 1], shape) * scaled[i] for i in idx
+            ]
+            while len(terms) > 1:
+                terms = [x + y for x, y in zip(terms[0::2], terms[1::2])]
+            out.append(jnp.where(inside, 0.0, tile) - terms[0])
         tiles = out
     return tiles
 
@@ -129,16 +179,16 @@
         for t, tile in enumerate(tiles):
             p[t * TILE : (t + 1) * TILE, :] = tile
         r[...] = -jnp.dot(p[...], a[ks, :], precision=HI, preferred_element_type=F32)
+        r[:, ks] = p[...]
 
         @pl.loop(0, steps)
         def _(i):
             rows = pl.ds(pl.multiple_of(i * BLOCK, BLOCK), BLOCK)
             c = a[rows, ks]
+            a[rows, ks] = jnp.zeros((BLOCK, BLOCK), F32)
             a[rows, :] = a[rows, :] - jnp.dot(c, r[...], precision=HI, preferred_element_type=F32)
-            a[rows, ks] = -jnp.dot(c, p[...], precision=HI, preferred_element_type=F32)
 
         a[ks, :] = r[...]
-        a[ks, ks] = p[...]
 
     fresh = refreshed[0] > 0
 
@@ -198,28 +248,60 @@
         for j in range(n):
             total = total + jnp.dot(got[j], inv[j * rw : (j + 1) * rw, :], preferred_element_type=F32)
         done[m // 2] = (total * step[m // 2]).astype(BF16)
-        for q in range(1, parts):
-            remote(
-                done.at[m // 2], done.at[m // 2], s2.at[q], r2.at[q], (me, (m + q) % parts)
-            ).start()
-        for q in range(1, parts):
-            remote(
-                done.at[m // 2], done.at[m // 2], s2.at[q], r2.at[q], (me, (m + q) % parts)
-            ).wait_send()
+
+    chunks = max(1, min(4, rw // 16))
+    size = rw // chunks
+
+    def hop(layer, c, way, where):
+        part = done.at[layer, pl.ds(c * size, size)]
+        return remote(part, part, s2.at[layer, way, c], r2.at[layer, c], (me, where))
+
+    up, down = m + 1, m - 1
+    for c in range(chunks):
+        for s in range(0, parts, 2):
+            layer = s // 2
+
+            @pl.when((m == s) & (up < parts))
+            def _():
+                hop(layer, c, 0, up).start()
+
+            @pl.when((m == s) & (down >= 0))
+            def _():
+                hop(layer, c, 1, down).start()
+
+    for c in range(chunks):
+        for s in range(0, parts, 2):
+            layer = s // 2
+
+            @pl.when(m != s)
+            def _():
+                hop(layer, c, 0, other).wait_recv()
+
+            @pl.when((m > s) & (up < parts))
+            def _():
+                hop(layer, c, 0, up).start()
+
+            @pl.when((m < s) & (down >= 0))
+            def _():
+                hop(layer, c, 1, down).start()
+
+    for c in range(chunks):
+        for s in range(0, parts, 2):
+            layer = s // 2
+
+            @pl.when((m >= s) & (up < parts))
+            def _():
+                hop(layer, c, 0, other).wait_send()
+
+            @pl.when((m <= s) & (down >= 0))
+            def _():
+                hop(layer, c, 1, other).wait_send()
 
     @pl.when(is_out == 1)
     def _():
         for s in range(n):
             j = (me + s) % n
             remote(b.at[j], got.at[me], s1.at[s], r1.at[s], (j, other)).wait_send()
-
-    for q in range(1, parts):
-        origin = (m - q + parts) % parts
-
-        @pl.when(origin % 2 == 0)
-        def _():
-            slot = origin // 2
-            remote(done.at[slot], done.at[slot], s2.at[q], r2.at[q], (me, origin)).wait_recv()
 
     out[...] = done[...]
 
@@ -239,7 +321,7 @@
             pltpu.VMEM((n, rw, rw), BF16),
             pltpu.VMEM((n, rw, rw), BF16),
             pltpu.VMEM((layers, rw, width), BF16),
-            dma((n,)), dma((n,)), dma((parts,)), dma((parts,)),
+            dma((n,)), dma((n,)), dma((layers, 2, 4)), dma((layers, 4)),
         ],
         compiler_params=pltpu.CompilerParams(
             collective_id=1, has_side_effects=True, vmem_limit_bytes=32 * 1024 * 1024
@@ -256,12 +338,16 @@
     width = layer_inputs.shape[2]
     count_all = tokens * n
     rw = width // n
-    xs = lax.dynamic_index_in_dim(layer_inputs, m // 2, 0, keepdims=False)
-    gs = lax.dynamic_index_in_dim(out_grads, m // 2, 0, keepdims=False)
-    even = m % 2 == 0
-    mine = jnp.where(even, xs, gs)
-    other = jnp.where(even, gs, xs).reshape(tokens, n, rw).transpose(1, 0, 2)
-    source, columns = gather(n, mine, other)
+    direct = rw % 128 == 0
+    if direct:
+        mine, other = layer_inputs, out_grads
+    else:
+        xs = lax.dynamic_index_in_dim(layer_inputs, m // 2, 0, keepdims=False)
+        gs = lax.dynamic_index_in_dim(out_grads, m // 2, 0, keepdims=False)
+        even = m % 2 == 0
+        mine = jnp.where(even, xs, gs)
+        other = jnp.where(even, gs, xs).reshape(tokens, n, rw).transpose(1, 0, 2)
+    source, columns = gather(n, direct, mine, other)
     source = source.reshape(count_all, width)
     columns = columns.reshape(count_all, rw)
     dims = (((0,), (0,)), ((), ()))

time: 285 us -> 170 us (0.60)
  Pallas kernels: 265 us -> 154 us
    pallas_call x1, Pallas kernels: 187 us -> 81 us  [invert(): pl.pallas_call(invert_kernel, out_shape=jax.ShapeDtypeStruct((width, widt...]
    pallas_call x1, Pallas kernels: 30.6 us -> 25.3 us  [apply(): pl.pallas_call(functools.partial(apply_kernel, n, parts), out_shape=jax.S...]
where the time goes in v2:
time: 170 us
  Pallas kernels  154 us (91%)
  matrix products  12 us (7%)
  local copies, waits for them, and re-layouts  3.29 us (2%)
    pallas_call x1, Pallas kernels, invert(): pl.pallas_call(invert_kernel, out_shape=jax.ShapeDtypeStruct((width, widt...  81 us
    pallas_call x1, Pallas kernels, gather(): pl.pallas_call(functools.partial(gather_kernel, n, direct), out_shape=[ja...  47.4 us
    pallas_call x1, Pallas kernels, apply(): pl.pallas_call(functools.partial(apply_kernel, n, parts), out_shape=jax.S...  25.3 us
    dot_general x1, matrix products, body(): lax.dot_general(source, source, dims, preferred_element_type=F32)  7.03 us
    dot_general x1, matrix products, body(): lax.dot_general(source, columns, dims, preferred_element_type=F32)  4.94 us

profile of v2, /device:TPU:0, one launch (start us, length us, event | category | flops | bytes accessed | tf_op | source)
XLA Modules:
  0.0 169.7 jit_solution(3931430039274169304)
XLA Ops:
  0.0 1.2 dynamic_slice.6
  1.9 1.2 dynamic_slice.7.shift
  3.1 47.4 %gather_sources.1 = (bf16[8,384,1024]{2,1,0:T(8,128)(2,1)}, bf16[8,384,128]{2,1,0:T(8,128)(2,1)}) custom-call(bf16[2,384,1024]{2,1,0:T(8,128)(2,1)} %a_ref.1, bf16[2,384,1024]{2,1,0:T(8,128)(2,1)} %b_ref.1), custom_call_target="tpu_custom_call" | custom-call | tf_op jit(solution)/shard_map/gather_sources/pallas_call | solution.py:88
  50.5 0.0 copy-start.2
  50.5 4.9 %fusion.1.grad = bf16[1024,128]{1,0:T(8,128)(2,1)S(1)} fusion(bf16[8,384,1024]{2,1,0:T(8,128)(2,1)} %get-tuple-element.7, bf16[8,384,128]{2,1,0:T(8,128)(2,1)} %get-tuple-element.8), kind=kOutput, calls=%fused_computation.3 | convolution fusion | flops 805568512 | bytes 7340032 | tf_op jit(solution)/shard_map/dot_general | solution.py:355
  55.5 0.0 copy-done.2
  55.5 0.0 copy-start
  55.5 7.0 %bitcast_multiply_fusion.factor = f32[1024,1024]{1,0:T(8,128)S(1)} fusion(bf16[8,384,1024]{2,1,0:T(8,128)(2,1)S(1)} %copy-done.2), kind=kOutput, calls=%fused_computation | convolution fusion | flops 6443499520 | bytes 10485760 | tf_op jit(solution)/shard_map/dot_general | solution.py:354
  62.5 0.0 copy-done
  62.5 0.0 copy-start.1
  62.6 81.0 %invert_damped.1.inv = bf16[1024,1024]{1,0:T(8,128)(2,1)S(1)} custom-call(s32[1]{0:T(128)S(6)} %convert_element_type.7.refreshed, f32[1]{0:T(128)} %dynamic_slice.7.shift, f32[1024,1024]{1,0:T(8,128)S(1)} %bitcast_multiply_fusion.factor, bf16[1024,1024]{1,0:T(8,128)(2,1)S(1)} %bitcast.13), custom_call_target="tpu_custom_call" | custom-call | tf_op jit(solution)/shard_map/invert_damped/pallas_call | solution.py:205
  143.6 0.0 copy-done.1
  143.6 25.3 %apply_inverses.1 = bf16[2,128,1024]{2,1,0:T(8,128)(2,1)S(1)} custom-call(bf16[1024,1024]{1,0:T(8,128)(2,1)S(1)} %invert_damped.1.inv, bf16[1024,128]{1,0:T(8,128)(2,1)S(1)} %fusion.1.grad, f32[2]{0:T(128)S(1)} %copy-done.1), custom_call_target="tpu_custom_call" | custom-call | tf_op jit(solution)/shard_map/apply_inverses/pallas_call | solution.py:315
  168.9 0.8 copy.12
Async XLA Ops:
  50.5 5.0 %copy-start.2 = (bf16[8,384,1024]{2,1,0:T(8,128)(2,1)S(1)}, bf16[8,384,1024]{2,1,0:T(8,128)(2,1)}, u32[]{:S(2)}) copy-start(bf16[8,384,1024]{2,1,0:T(8,128)(2,1)} %get-tuple-element.7) | copy-start | bytes 18874372
  55.5 7.0 %copy-start = (bf16[1,1024,1024]{2,1,0:T(8,128)(2,1)S(1)}, bf16[1,1024,1024]{2,1,0:T(8,128)(2,1)}, u32[]{:S(2)}) copy-start(bf16[1,1024,1024]{2,1,0:T(8,128)(2,1)} %param.10) | copy-start | bytes 6291460
  62.5 81.0 %copy-start.1 = (f32[2]{0:T(128)S(1)}, f32[2]{0:T(128)}, u32[]{:S(2)}) copy-start(f32[2]{0:T(128)} %step.1) | copy-start | bytes 28

commit v3 on v2

--- a/solution.py
+++ b/solution.py
@@ -11,6 +11,7 @@
 MESH = pl.DeviceIdType.MESH
 HI = lax.Precision.HIGHEST
 BLOCK = 128
+WIDE = 256
 TILE = 8
 
 
@@ -159,7 +160,14 @@
     return tiles
 
 
-def invert_kernel(refreshed, shift, factor, kept, out, a, r, p):
+def split(x):
+    first = x.astype(BF16)
+    left = x - first.astype(F32)
+    second = left.astype(BF16)
+    return first, second, (left - second.astype(F32)).astype(BF16)
+
+
+def invert_kernel(refreshed, shift, factor, kept, out, a, r, p, left, right):
     width = factor.shape[0]
     steps = width // BLOCK
     row_id = lax.broadcasted_iota(jnp.int32, (BLOCK, width), 0)
@@ -181,12 +189,17 @@
         r[...] = -jnp.dot(p[...], a[ks, :], precision=HI, preferred_element_type=F32)
         r[:, ks] = p[...]
 
-        @pl.loop(0, steps)
+        c = split(a[:, ks])
+        q = split(r[...])
+        for t, (i, j) in enumerate(((0, 2), (2, 0), (1, 1), (0, 1), (1, 0), (0, 0))):
+            left[:, t * BLOCK : (t + 1) * BLOCK] = c[i]
+            right[t * BLOCK : (t + 1) * BLOCK, :] = q[j]
+        a[:, ks] = jnp.zeros((width, BLOCK), F32)
+
+        @pl.loop(0, width // WIDE)
         def _(i):
-            rows = pl.ds(pl.multiple_of(i * BLOCK, BLOCK), BLOCK)
-            c = a[rows, ks]
-            a[rows, ks] = jnp.zeros((BLOCK, BLOCK), F32)
-            a[rows, :] = a[rows, :] - jnp.dot(c, r[...], precision=HI, preferred_element_type=F32)
+            cols = pl.ds(pl.multiple_of(i * WIDE, WIDE), WIDE)
+            a[:, cols] = a[:, cols] - jnp.dot(left[...], right[:, cols], preferred_element_type=F32)
 
         a[ks, :] = r[...]
 
@@ -211,6 +224,8 @@
             pltpu.VMEM((width, width), F32),
             pltpu.VMEM((BLOCK, width), F32),
             pltpu.VMEM((BLOCK, BLOCK), F32),
+            pltpu.VMEM((width, 6 * BLOCK), BF16),
+            pltpu.VMEM((6 * BLOCK, width), BF16),
         ],
         compiler_params=pltpu.CompilerParams(vmem_limit_bytes=40 * 1024 * 1024),
         name="invert_damped",

time: 170 us -> 158 us (0.929)
  Pallas kernels: 154 us -> 142 us
    pallas_call x1, Pallas kernels: 81 us -> 68.8 us  [invert(): pl.pallas_call(invert_kernel, out_shape=jax.ShapeDtypeStruct((width, widt...]
where the time goes in v3:
time: 158 us
  Pallas kernels  142 us (90%)
  matrix products  12 us (8%)
  local copies, waits for them, and re-layouts  3.29 us (2%)
    pallas_call x1, Pallas kernels, invert(): pl.pallas_call(invert_kernel, out_shape=jax.ShapeDtypeStruct((width, widt...  68.8 us
    pallas_call x1, Pallas kernels, gather(): pl.pallas_call(functools.partial(gather_kernel, n, direct), out_shape=[ja...  47.4 us
    pallas_call x1, Pallas kernels, apply(): pl.pallas_call(functools.partial(apply_kernel, n, parts), out_shape=jax.S...  25.4 us
    dot_general x1, matrix products, body(): lax.dot_general(source, source, dims, preferred_element_type=F32)  7.03 us
    dot_general x1, matrix products, body(): lax.dot_general(source, columns, dims, preferred_element_type=F32)  4.94 us

profile of v3, /device:TPU:0, one launch (start us, length us, event | category | flops | bytes accessed | tf_op | source)
XLA Modules:
  0.0 157.6 jit_solution(17045430219473382984)
XLA Ops:
  0.0 1.2 dynamic_slice.6
  1.9 1.2 dynamic_slice.7.shift
  3.1 47.4 %gather_sources.1 = (bf16[8,384,1024]{2,1,0:T(8,128)(2,1)}, bf16[8,384,128]{2,1,0:T(8,128)(2,1)}) custom-call(bf16[2,384,1024]{2,1,0:T(8,128)(2,1)} %a_ref.1, bf16[2,384,1024]{2,1,0:T(8,128)(2,1)} %b_ref.1), custom_call_target="tpu_custom_call" | custom-call | tf_op jit(solution)/shard_map/gather_sources/pallas_call | solution.py:89
  50.5 0.0 copy-start.2
  50.5 4.9 %fusion.1.grad = bf16[1024,128]{1,0:T(8,128)(2,1)S(1)} fusion(bf16[8,384,1024]{2,1,0:T(8,128)(2,1)} %get-tuple-element.7, bf16[8,384,128]{2,1,0:T(8,128)(2,1)} %get-tuple-element.8), kind=kOutput, calls=%fused_computation.3 | convolution fusion | flops 805568512 | bytes 7340032 | tf_op jit(solution)/shard_map/dot_general | solution.py:370
  55.5 0.0 copy-done.2
  55.5 0.0 copy-start
  55.5 7.0 %bitcast_multiply_fusion.factor = f32[1024,1024]{1,0:T(8,128)S(1)} fusion(bf16[8,384,1024]{2,1,0:T(8,128)(2,1)S(1)} %copy-done.2), kind=kOutput, calls=%fused_computation | convolution fusion | flops 6443499520 | bytes 10485760 | tf_op jit(solution)/shard_map/dot_general | solution.py:369
  62.5 0.0 copy-done
  62.5 0.0 copy-start.1
  62.6 68.8 %invert_damped.1.inv = bf16[1024,1024]{1,0:T(8,128)(2,1)S(1)} custom-call(s32[1]{0:T(128)S(6)} %convert_element_type.7.refreshed, f32[1]{0:T(128)} %dynamic_slice.7.shift, f32[1024,1024]{1,0:T(8,128)S(1)} %bitcast_multiply_fusion.factor, bf16[1024,1024]{1,0:T(8,128)(2,1)S(1)} %bitcast.13), custom_call_target="tpu_custom_call" | custom-call | tf_op jit(solution)/shard_map/invert_damped/pallas_call | solution.py:218
  131.4 0.0 copy-done.1
  131.4 25.4 %apply_inverses.1 = bf16[2,128,1024]{2,1,0:T(8,128)(2,1)S(1)} custom-call(bf16[1024,1024]{1,0:T(8,128)(2,1)S(1)} %invert_damped.1.inv, bf16[1024,128]{1,0:T(8,128)(2,1)S(1)} %fusion.1.grad, f32[2]{0:T(128)S(1)} %copy-done.1), custom_call_target="tpu_custom_call" | custom-call | tf_op jit(solution)/shard_map/apply_inverses/pallas_call | solution.py:330
  156.8 0.8 copy.12
Async XLA Ops:
  50.5 5.0 %copy-start.2 = (bf16[8,384,1024]{2,1,0:T(8,128)(2,1)S(1)}, bf16[8,384,1024]{2,1,0:T(8,128)(2,1)}, u32[]{:S(2)}) copy-start(bf16[8,384,1024]{2,1,0:T(8,128)(2,1)} %get-tuple-element.7) | copy-start | bytes 18874372
  55.5 7.0 %copy-start = (bf16[1,1024,1024]{2,1,0:T(8,128)(2,1)S(1)}, bf16[1,1024,1024]{2,1,0:T(8,128)(2,1)}, u32[]{:S(2)}) copy-start(bf16[1,1024,1024]{2,1,0:T(8,128)(2,1)} %param.10) | copy-start | bytes 6291460
  62.5 68.8 %copy-start.1 = (f32[2]{0:T(128)S(1)}, f32[2]{0:T(128)}, u32[]{:S(2)}) copy-start(f32[2]{0:T(128)} %step.1) | copy-start | bytes 28

commit v4 on v3

--- a/solution.py
+++ b/solution.py
@@ -83,11 +83,109 @@
     pltpu.make_async_copy(gy.at[me], gy.at[me], loc.at[1]).wait()
 
 
+def square_gather_kernel(n, a_ref, b_ref, gx, gy, loc, s1, r1, s2, r2, s3, r3):
+    me = lax.axis_index("dp")
+    m = lax.axis_index("mp")
+    beside = m + 1 - 2 * (m % 2)
+    layer = m // 2
+    pair, side = me // 2, me % 2
+    px = pair + 1 - 2 * (pair % 2)
+    py = (pair + 2) % 4
+    pd = (px + 2) % 4
+    sibling = pair * 2 + 1 - side
+    near_x, near_y, far = px * 2 + side, py * 2 + side, pd * 2 + side
+    half = gx.shape[1] // 2
+    rw = gy.shape[2]
+    cols = pl.ds(pl.multiple_of(me * rw, rw), rw)
+    barrier = pltpu.get_barrier_semaphore()
+    for s in range(1, n):
+        pl.semaphore_signal(barrier, inc=1, device_id=((me + s) % n, m), device_id_type=MESH)
+    pl.semaphore_signal(barrier, inc=1, device_id=(me, beside), device_id_type=MESH)
+    pl.semaphore_wait(barrier, n)
+
+    def begin(x):
+        remote(x, gx.at[me], s1.at[1], r1.at[1], (near_x, m)).start()
+        remote(x, gx.at[me], s1.at[2], r1.at[2], (near_y, m)).start()
+        remote(x, gx.at[me], s1.at[0], r1.at[0], (sibling, m)).start()
+        pltpu.make_async_copy(x, gx.at[me], loc.at[0]).start()
+
+    @pl.when(m % 2 == 0)
+    def _():
+        begin(a_ref.at[layer])
+        remote(a_ref.at[layer, :, cols], gy.at[me], s3.at[0], r3.at[0], (me, beside)).start()
+
+    @pl.when(m % 2 == 1)
+    def _():
+        begin(b_ref.at[layer])
+
+    def whole(origin):
+        return gx.at[origin]
+
+    def part(origin, h):
+        return gx.at[origin, pl.ds(h * half, half)]
+
+    def arrive(block, sems, k):
+        remote(block, block, s1.at[0], sems.at[k], (sibling, m)).wait_recv()
+
+    def forward(block, k, peer):
+        remote(block, block, s2.at[k], r2.at[k], (peer, m)).start()
+
+    def columns(e, origin):
+        @pl.when(m % 2 == 0)
+        def _():
+            remote(gx.at[origin, :, cols], gy.at[origin], s3.at[e], r3.at[e], (me, beside)).start()
+
+    arrive(whole(sibling), r1, 0)
+    columns(1, sibling)
+    arrive(whole(near_x), r1, 1)
+    forward(part(near_x, 0), 5, near_y)
+    forward(whole(near_x), 1, sibling)
+    columns(2, near_x)
+    arrive(whole(near_y), r1, 2)
+    forward(part(near_y, 1), 6, near_x)
+    forward(whole(near_y), 2, sibling)
+    columns(4, near_y)
+    other_x, other_y, other_far = px * 2 + 1 - side, py * 2 + 1 - side, pd * 2 + 1 - side
+    arrive(whole(other_x), r2, 1)
+    columns(3, other_x)
+    arrive(whole(other_y), r2, 2)
+    columns(5, other_y)
+    arrive(part(far, 0), r2, 5)
+    forward(part(far, 0), 3, sibling)
+    arrive(part(far, 1), r2, 6)
+    forward(part(far, 1), 4, sibling)
+    columns(6, far)
+    arrive(part(other_far, 0), r2, 3)
+    arrive(part(other_far, 1), r2, 4)
+    columns(7, other_far)
+    order = (me, sibling, near_x, other_x, near_y, other_y, far, other_far)
+
+    @pl.when(m % 2 == 1)
+    def _():
+        for e, origin in enumerate(order):
+            remote(gy.at[origin], gy.at[origin], s3.at[e], r3.at[e], (me, beside)).wait_recv()
+
+    @pl.when(m % 2 == 0)
+    def _():
+        for e, origin in enumerate(order):
+            remote(gx.at[origin, :, cols], gy.at[origin], s3.at[e], r3.at[e], (me, beside)).wait_send()
+
+    for k in range(3):
+        remote(whole(me), whole(me), s1.at[k], r1.at[k], (sibling, m)).wait_send()
+    for k, block in (
+        (1, whole(near_x)), (2, whole(near_y)), (3, part(far, 0)), (4, part(far, 1)),
+        (5, part(near_x, 0)), (6, part(near_y, 1)),
+    ):
+        remote(block, block, s2.at[k], r2.at[k], (sibling, m)).wait_send()
+    pltpu.make_async_copy(whole(me), whole(me), loc.at[0]).wait()
+
+
 def gather(n, direct, x, y):
+    square = direct and n == 8 and x.shape[-2] % 32 == 0
     any_space = pl.BlockSpec(memory_space=pl.ANY)
     dma = pltpu.SemaphoreType.DMA
     return pl.pallas_call(
-        functools.partial(gather_kernel, n, direct),
+        functools.partial(square_gather_kernel, n) if square else functools.partial(gather_kernel, n, direct),
         out_shape=[
             jax.ShapeDtypeStruct((n,) + x.shape[-2:], x.dtype),
             jax.ShapeDtypeStruct((n, x.shape[-2], x.shape[-1] // n), y.dtype),

time: 158 us -> 148 us (0.937)
  Pallas kernels: 142 us -> 131 us
    pallas_call x1, Pallas kernels: 47.4 us -> 38 us  [gather(): pl.pallas_call(functools.partial(square_gather_kernel, n) if square else...]
where the time goes in v4:
time: 148 us; the launch traced here: 147 us
  Pallas kernels  131 us (89%)
  matrix products  12 us (8%)
  local copies, waits for them, and re-layouts  3.29 us (2%)
    pallas_call x1, Pallas kernels, invert(): pl.pallas_call(invert_kernel, out_shape=jax.ShapeDtypeStruct((width, widt...  68.8 us
    pallas_call x1, Pallas kernels, gather(): pl.pallas_call(functools.partial(square_gather_kernel, n) if square else...  38 us
    pallas_call x1, Pallas kernels, apply(): pl.pallas_call(functools.partial(apply_kernel, n, parts), out_shape=jax.S...  24.7 us
    dot_general x1, matrix products, body(): lax.dot_general(source, source, dims, preferred_element_type=F32)  7.03 us
    dot_general x1, matrix products, body(): lax.dot_general(source, columns, dims, preferred_element_type=F32)  4.94 us

profile of v4, /device:TPU:0, one launch (start us, length us, event | category | flops | bytes accessed | tf_op | source)
XLA Modules:
  0.0 147.5 jit_solution(1246919770521912910)
XLA Ops:
  0.0 1.2 dynamic_slice.6
  1.9 1.2 dynamic_slice.7.shift
  3.1 38.0 %gather_sources.1 = (bf16[8,384,1024]{2,1,0:T(8,128)(2,1)}, bf16[8,384,128]{2,1,0:T(8,128)(2,1)}) custom-call(bf16[2,384,1024]{2,1,0:T(8,128)(2,1)} %a_ref.1, bf16[2,384,1024]{2,1,0:T(8,128)(2,1)} %b_ref.1), custom_call_target="tpu_custom_call" | custom-call | tf_op jit(solution)/shard_map/gather_sources/pallas_call | solution.py:187
  41.1 0.0 copy-start.2
  41.1 4.9 %fusion.1.grad = bf16[1024,128]{1,0:T(8,128)(2,1)S(1)} fusion(bf16[8,384,1024]{2,1,0:T(8,128)(2,1)} %get-tuple-element.7, bf16[8,384,128]{2,1,0:T(8,128)(2,1)} %get-tuple-element.8), kind=kOutput, calls=%fused_computation.3 | convolution fusion | flops 805568512 | bytes 7340032 | tf_op jit(solution)/shard_map/dot_general | solution.py:468
  46.1 0.0 copy-done.2
  46.1 0.0 copy-start
  46.1 7.0 %bitcast_multiply_fusion.factor = f32[1024,1024]{1,0:T(8,128)S(1)} fusion(bf16[8,384,1024]{2,1,0:T(8,128)(2,1)S(1)} %copy-done.2), kind=kOutput, calls=%fused_computation | convolution fusion | flops 6443499520 | bytes 10485760 | tf_op jit(solution)/shard_map/dot_general | solution.py:467
  53.1 0.0 copy-done
  53.1 0.0 copy-start.1
  53.1 68.8 %invert_damped.1.inv = bf16[1024,1024]{1,0:T(8,128)(2,1)S(1)} custom-call(s32[1]{0:T(128)S(6)} %convert_element_type.7.refreshed, f32[1]{0:T(128)} %dynamic_slice.7.shift, f32[1024,1024]{1,0:T(8,128)S(1)} %bitcast_multiply_fusion.factor, bf16[1024,1024]{1,0:T(8,128)(2,1)S(1)} %bitcast.13), custom_call_target="tpu_custom_call" | custom-call | tf_op jit(solution)/shard_map/invert_damped/pallas_call | solution.py:316
  122.0 0.0 copy-done.1
  122.0 24.7 %apply_inverses.1 = bf16[2,128,1024]{2,1,0:T(8,128)(2,1)S(1)} custom-call(bf16[1024,1024]{1,0:T(8,128)(2,1)S(1)} %invert_damped.1.inv, bf16[1024,128]{1,0:T(8,128)(2,1)S(1)} %fusion.1.grad, f32[2]{0:T(128)S(1)} %copy-done.1), custom_call_target="tpu_custom_call" | custom-call | tf_op jit(solution)/shard_map/apply_inverses/pallas_call | solution.py:428
  146.7 0.8 copy.12
Async XLA Ops:
  41.1 5.0 %copy-start.2 = (bf16[8,384,1024]{2,1,0:T(8,128)(2,1)S(1)}, bf16[8,384,1024]{2,1,0:T(8,128)(2,1)}, u32[]{:S(2)}) copy-start(bf16[8,384,1024]{2,1,0:T(8,128)(2,1)} %get-tuple-element.7) | copy-start | bytes 18874372
  46.1 7.0 %copy-start = (bf16[1,1024,1024]{2,1,0:T(8,128)(2,1)S(1)}, bf16[1,1024,1024]{2,1,0:T(8,128)(2,1)}, u32[]{:S(2)}) copy-start(bf16[1,1024,1024]{2,1,0:T(8,128)(2,1)} %param.10) | copy-start | bytes 6291460
  53.1 68.8 %copy-start.1 = (f32[2]{0:T(128)S(1)}, f32[2]{0:T(128)}, u32[]{:S(2)}) copy-start(f32[2]{0:T(128)} %step.1) | copy-start | bytes 28

commit v5 on v4

--- a/solution.py
+++ b/solution.py
@@ -265,16 +265,19 @@
     return first, second, (left - second.astype(F32)).astype(BF16)
 
 
-def invert_kernel(refreshed, shift, factor, kept, out, a, r, p, left, right):
+def invert_kernel(n, owners, damping, factor, kept, out, a, r, p, left, right):
     width = factor.shape[0]
     steps = width // BLOCK
+    mine = lax.axis_index("mp")
+    shift = damping[mine]
+    fresh = owners[mine] < n
     row_id = lax.broadcasted_iota(jnp.int32, (BLOCK, width), 0)
     col_id = lax.broadcasted_iota(jnp.int32, (BLOCK, width), 1)
 
     @pl.loop(0, steps)
     def _(i):
         rows = pl.ds(pl.multiple_of(i * BLOCK, BLOCK), BLOCK)
-        a[rows, :] = factor[rows, :] + jnp.where(row_id + i * BLOCK == col_id, shift[0], 0.0)
+        a[rows, :] = factor[rows, :] + jnp.where(row_id + i * BLOCK == col_id, shift, 0.0)
 
     @pl.loop(0, steps)
     def _(k):
@@ -301,20 +304,18 @@
 
         a[ks, :] = r[...]
 
-    fresh = refreshed[0] > 0
-
     @pl.loop(0, steps)
     def _(i):
         rows = pl.ds(pl.multiple_of(i * BLOCK, BLOCK), BLOCK)
         out[rows, :] = jnp.where(fresh, -a[rows, :], kept[rows, :].astype(F32)).astype(BF16)
 
 
-def invert(refreshed, shift, factor, kept):
+def invert(n, owners, damping, factor, kept):
     width = factor.shape[0]
     smem = pl.BlockSpec(memory_space=pltpu.SMEM)
     vmem = pl.BlockSpec(memory_space=pltpu.VMEM)
     return pl.pallas_call(
-        invert_kernel,
+        functools.partial(invert_kernel, n),
         out_shape=jax.ShapeDtypeStruct((width, width), BF16),
         in_specs=[smem, smem, vmem, vmem],
         out_specs=vmem,
@@ -327,7 +328,7 @@
         ],
         compiler_params=pltpu.CompilerParams(vmem_limit_bytes=40 * 1024 * 1024),
         name="invert_damped",
-    )(refreshed, shift, factor, kept)
+    )(owners, damping, factor, kept)
 
 
 def apply_kernel(n, parts, inv, grad, step, out, b, got, done, s1, r1, s2, r2):
@@ -344,7 +345,10 @@
         pl.semaphore_signal(barrier, inc=1, device_id=(me, (m + q) % parts), device_id_type=MESH)
     pl.semaphore_wait(barrier, n + parts - 1)
 
-    b[...] = jnp.dot(inv[...], grad[...], preferred_element_type=F32).astype(BF16).reshape(n, rw, rw)
+    product = lax.dot_general(
+        inv[...], grad[...], (((1,), (1,)), ((), ())), preferred_element_type=F32
+    )
+    b[...] = product.astype(BF16).reshape(n, rw, rw)
     for s in range(n):
         j = (me + s) % n
 
@@ -465,10 +469,8 @@
     columns = columns.reshape(count_all, rw)
     dims = (((0,), (0,)), ((), ()))
     factor = lax.dot_general(source, source, dims, preferred_element_type=F32) / count_all
-    grad = (lax.dot_general(source, columns, dims, preferred_element_type=F32) / count_all).astype(BF16)
-    refreshed = (owners[m] < n).astype(jnp.int32).reshape(1)
-    shift = damping[m].reshape(1)
-    inverse = invert(refreshed, shift, factor, old_inverse[0])
+    grad = (lax.dot_general(columns, source, dims, preferred_element_type=F32) / count_all).astype(BF16)
+    inverse = invert(n, owners, damping, factor, old_inverse[0])
     return apply(n, parts, inverse, grad, step_size)
 
 

time: 148 us -> 145 us (0.980)
  local copies, waits for them, and re-layouts: 3.29 us -> 1.43 us
    dynamic_slice x2 -> x0, local copies, waits for them, and re-layouts: 2.48 us -> none  [the longest x1 1.24 us: body(): shift = damping[m].reshape(1)]
where the time goes in v5:
time: 145 us; the launch traced here: 144 us
  Pallas kernels  131 us (90%)
  matrix products  11.2 us (8%)
    pallas_call x1, Pallas kernels, invert(): pl.pallas_call(functools.partial(invert_kernel, n), out_shape=jax.ShapeDt...  68.6 us
    pallas_call x1, Pallas kernels, gather(): pl.pallas_call(functools.partial(square_gather_kernel, n) if square else...  38 us
    pallas_call x1, Pallas kernels, apply(): pl.pallas_call(functools.partial(apply_kernel, n, parts), out_shape=jax.S...  24.7 us
    dot_general x1, matrix products, body(): lax.dot_general(source, source, dims, preferred_element_type=F32)  7.03 us
    dot_general x1, matrix products, body(): lax.dot_general(columns, source, dims, preferred_element_type=F32)  4.18 us

profile of v5, /device:TPU:0, one launch (start us, length us, event | category | flops | bytes accessed | tf_op | source)
XLA Modules:
  0.0 143.9 jit_solution(2277150063907651615)
XLA Ops:
  0.0 38.0 %gather_sources.1 = (bf16[8,384,1024]{2,1,0:T(8,128)(2,1)}, bf16[8,384,128]{2,1,0:T(8,128)(2,1)}) custom-call(bf16[2,384,1024]{2,1,0:T(8,128)(2,1)} %a_ref.1, bf16[2,384,1024]{2,1,0:T(8,128)(2,1)} %b_ref.1), custom_call_target="tpu_custom_call" | custom-call | tf_op jit(solution)/shard_map/gather_sources/pallas_call | solution.py:187
  38.0 0.0 copy-start.4
  38.0 4.2 %fusion.1.grad = bf16[128,1024]{1,0:T(8,128)(2,1)S(1)} fusion(bf16[8,384,128]{2,1,0:T(8,128)(2,1)} %get-tuple-element.8, bf16[8,384,1024]{2,1,0:T(8,128)(2,1)} %get-tuple-element.7), kind=kOutput, calls=%fused_computation.3 | convolution fusion | flops 805568512 | bytes 7340032 | tf_op jit(solution)/shard_map/dot_general | solution.py:472
  42.2 0.6 copy-done.4
  42.8 0.0 copy-start
  42.8 0.0 copy-start.1
  42.8 0.0 copy-start.2
  42.8 7.0 %bitcast_multiply_fusion.factor = f32[1024,1024]{1,0:T(8,128)S(1)} fusion(bf16[8,384,1024]{2,1,0:T(8,128)(2,1)S(1)} %copy-done.4), kind=kOutput, calls=%fused_computation | convolution fusion | flops 6443499520 | bytes 10485760 | tf_op jit(solution)/shard_map/dot_general | solution.py:471
  49.8 0.0 copy-done
  49.8 0.0 copy-done.1
  49.8 0.0 copy-done.2
  49.9 0.0 copy-start.3
  49.9 68.6 %invert_damped.1.inv = bf16[1024,1024]{1,0:T(8,128)(2,1)S(1)} custom-call(s32[4]{0:T(128)S(1)} %copy-done.1, f32[4]{0:T(128)S(1)} %copy-done.2, f32[1024,1024]{1,0:T(8,128)S(1)} %bitcast_multiply_fusion.factor, bf16[1024,1024]{1,0:T(8,128)(2,1)S(1)} %bitcast.13), custom_call_target="tpu_custom_call" | custom-call | tf_op jit(solution)/shard_map/invert_damped/pallas_call | solution.py:317
  118.4 0.0 copy-done.3
  118.4 24.7 %apply_inverses.1 = bf16[2,128,1024]{2,1,0:T(8,128)(2,1)S(1)} custom-call(bf16[1024,1024]{1,0:T(8,128)(2,1)S(1)} %invert_damped.1.inv, bf16[128,1024]{1,0:T(8,128)(2,1)S(1)} %fusion.1.grad, f32[2]{0:T(128)S(1)} %copy-done.3), custom_call_target="tpu_custom_call" | custom-call | tf_op jit(solution)/shard_map/apply_inverses/pallas_call | solution.py:432
  143.1 0.8 copy.12
Async XLA Ops:
  38.0 4.8 %copy-start.4 = (bf16[8,384,1024]{2,1,0:T(8,128)(2,1)S(1)}, bf16[8,384,1024]{2,1,0:T(8,128)(2,1)}, u32[]{:S(2)}) copy-start(bf16[8,384,1024]{2,1,0:T(8,128)(2,1)} %get-tuple-element.7) | copy-start | bytes 18874372
  42.8 7.0 %copy-start = (bf16[1,1024,1024]{2,1,0:T(8,128)(2,1)S(1)}, bf16[1,1024,1024]{2,1,0:T(8,128)(2,1)}, u32[]{:S(2)}) copy-start(bf16[1,1024,1024]{2,1,0:T(8,128)(2,1)} %param.10) | copy-start | bytes 6291460
  42.8 7.0 %copy-start.1 = (s32[4]{0:T(128)S(1)}, s32[4]{0:T(128)}, u32[]{:S(2)}) copy-start(s32[4]{0:T(128)} %owners.1) | copy-start | bytes 52
  42.8 7.1 %copy-start.2 = (f32[4]{0:T(128)S(1)}, f32[4]{0:T(128)}, u32[]{:S(2)}) copy-start(f32[4]{0:T(128)} %damping.1) | copy-start | bytes 52
  49.9 68.6 %copy-start.3 = (f32[2]{0:T(128)S(1)}, f32[2]{0:T(128)}, u32[]{:S(2)}) copy-start(f32[2]{0:T(128)} %step.1) | copy-start | bytes 28
